TPU v7x, 512 devices: a whole 4x4x16 slice. The times are simulated.
512 devices in a mesh: gx: 32 (over x, y, core), gy: 16 (over z).
Axes of the slice: x: 4, y: 4, z: 16, core: 2. Of those that a mesh axis runs over, the one named last changes fastest.
Arguments:
- right_side: float32 [2, 512, 2048], P(None, 'gx', 'gy'), may hold values from -160 to 160
- conductivity: float32 [512, 2048], P('gx', 'gy'), may hold values from 0.2 to 5
- leaf_inverse: float32 [128, 64, 128, 128], P('gx', 'gy'), may hold values from -1 to 4, as said below
- front_basis: float32 [512, 2048, 128], P('gx', 'gy'), may hold values from -0.25 to 0.25
- leaf_transfer: float32 [32, 16, 128, 128], P('gx', 'gy'), may hold values from -0.4375 to 0.4375
- node_transfer: float32 [32, 16, 8, 128, 128], P('gx', 'gy'), may hold values from -1 to 1, as said below
- leaf_front: float32 [32, 16, 128, 128], P('gx', 'gy'), may hold values from -1 to 1, as said below
- node_front: float32 [32, 16, 9, 128, 128], P('gx', 'gy'), may hold values from -1 to 1, as said below
Outputs:
- solution: float32 [2, 512, 2048], P(None, 'gx', 'gy')
- residual: float32 [2, 512, 2048], P(None, 'gx', 'gy')
- direction: float32 [2, 512, 2048], P(None, 'gx', 'gy')
Inputs may be any that keep to these rules, and one draw needn't show every extreme that they name: `leaf_inverse`: every block is symmetric and positive definite. `leaf_front`: every matrix is symmetric and positive definite. `node_front`: every matrix is symmetric and positive definite; entry h - 1 is the same for all tiles covered by one node of level h. `node_transfer`: entry h - 1 is the same for all tiles covered by one node of level h.
All inputs are finite; a program needn't handle non-finite values.
Results may differ from a plain program's by a relative error of at most 0.0001.
Values sent between devices are 32-bit elements; how exact they have to be, the bound alone decides.
A program may use at most 64 MiB of HBM per device.

v0:
```python
from functools import partial
import jax
import jax.numpy as jnp
from jax import lax
from jax.sharding import PartitionSpec as P

LBX = 4
LBY = 32
HIGHEST = lax.Precision.HIGHEST


def extended(cells, sides, width):
    for axis, dim in sides:
        count = lax.axis_size(axis)
        ends = count - 1
        head = lax.slice_in_dim(cells, 0, width, axis=dim)
        tail = lax.slice_in_dim(cells, cells.shape[dim] - width, cells.shape[dim], axis=dim)
        cells = jnp.concatenate(
            [
                lax.ppermute(tail, axis, [(i, (i + 1) % count) for i in range(ends)]),
                cells,
                lax.ppermute(head, axis, [((i + 1) % count, i) for i in range(ends)]),
            ],
            axis=dim,
        )
    return cells


def from_partner(value, axis, distance):
    mask = 2**distance
    pairs = [(source, source ^ mask) for source in range(lax.axis_size(axis))]
    return lax.ppermute(value, axis, pairs)


def operate_padded(padded, padded_k):
    extent_x = padded.shape[1] - 2
    extent_y = padded.shape[2] - 2
    center = padded[:, 1:-1, 1:-1]
    center_k = padded_k[1:-1, 1:-1]
    summed = jnp.zeros_like(center)
    for offset_x, offset_y in ((2, 1), (0, 1), (1, 2), (1, 0)):
        beside = padded[:, offset_x : offset_x + extent_x, offset_y : offset_y + extent_y]
        beside_k = padded_k[offset_x : offset_x + extent_x, offset_y : offset_y + extent_y]
        summed = summed + 0.5 * (center_k + beside_k) * (center - beside)
    return summed


def stencil(values, conductivity):
    stacked = jnp.concatenate([values, conductivity[None]], axis=0)
    padded = extended(stacked, (("gx", 1), ("gy", 2)), 1)
    return operate_padded(padded[:-1], padded[-1])


def leaf_apply(values, leaf_inverse):
    count_s, extent_x, extent_y = values.shape
    blocks_x = extent_x // LBX
    blocks_y = extent_y // LBY
    grouped = values.reshape(count_s, blocks_x, LBX, blocks_y, LBY).transpose(0, 1, 3, 2, 4)
    grouped = grouped.reshape(count_s, blocks_x, blocks_y, LBX * LBY)
    mapped = jnp.einsum("xyij,sxyj->sxyi", leaf_inverse, grouped, precision=HIGHEST)
    mapped = mapped.reshape(count_s, blocks_x, blocks_y, LBX, LBY).transpose(0, 1, 3, 2, 4)
    return mapped.reshape(count_s, extent_x, extent_y)


def spread_tree(coeffs, leaf_transfer, node_transfer, leaf_front, node_front):
    levels = lax.axis_size(("gx", "gy")).bit_length() - 1
    leaf_t = leaf_transfer[0, 0]
    leaf_f = leaf_front[0, 0]
    node_t = node_transfer[0, 0]
    node_f = node_front[0, 0]
    uppers = [coeffs]
    moving = jnp.dot(coeffs, leaf_t, precision=HIGHEST)
    for height in range(1, levels + 1):
        partner = from_partner(moving, ("gx", "gy"), height - 1)
        summed = moving + partner
        uppers.append(summed)
        if height < levels:
            moving = jnp.dot(summed, node_t[height - 1], precision=HIGHEST)
    downward = jnp.dot(uppers[levels], node_f[levels - 1], precision=HIGHEST)
    for height in range(levels, 1, -1):
        downward = jnp.dot(downward, node_t[height - 2].T, precision=HIGHEST) + jnp.dot(
            uppers[height - 1], node_f[height - 2], precision=HIGHEST
        )
    return jnp.dot(downward, leaf_t.T, precision=HIGHEST) + jnp.dot(
        coeffs, leaf_f, precision=HIGHEST
    )


def precondition(
    values, leaf_inverse, front_basis, leaf_transfer, node_transfer, leaf_front, node_front
):
    near = leaf_apply(values, leaf_inverse)
    coeffs = jnp.einsum("sab,abk->sk", values, front_basis, precision=HIGHEST)
    spread = spread_tree(coeffs, leaf_transfer, node_transfer, leaf_front, node_front)
    return near + jnp.einsum("sk,abk->sab", spread, front_basis, precision=HIGHEST)


def on_device(
    right_side,
    conductivity,
    leaf_inverse,
    front_basis,
    leaf_transfer,
    node_transfer,
    leaf_front,
    node_front,
):
    apply_inverse = partial(
        precondition,
        leaf_inverse=leaf_inverse,
        front_basis=front_basis,
        leaf_transfer=leaf_transfer,
        node_transfer=node_transfer,
        leaf_front=leaf_front,
        node_front=node_front,
    )
    first_z = apply_inverse(right_side)
    local_rz = jnp.sum(right_side * first_z, axis=(1, 2))
    rz_old = lax.psum(local_rz, ("gx", "gy"))
    applied = stencil(first_z, conductivity)
    curvature = lax.psum(jnp.sum(first_z * applied, axis=(1, 2)), ("gx", "gy"))
    step_size = (rz_old / curvature)[:, None, None]
    solution = step_size * first_z
    residual = right_side - step_size * applied
    second_z = apply_inverse(residual)
    rz_new = lax.psum(jnp.sum(residual * second_z, axis=(1, 2)), ("gx", "gy"))
    direction = second_z + (rz_new / rz_old)[:, None, None] * first_z
    return (solution, residual, direction)


def solution(mesh):
    return jax.shard_map(
        on_device,
        mesh=mesh,
        in_specs=(
            P(None, "gx", "gy"),
            P("gx", "gy"),
            P("gx", "gy", None, None),
            P("gx", "gy", None),
            P("gx", "gy", None, None),
            P("gx", "gy", None, None, None),
            P("gx", "gy", None, None),
            P("gx", "gy", None, None, None),
        ),
        out_specs=(P(None, "gx", "gy"), P(None, "gx", "gy"), P(None, "gx", "gy")),
        check_vma=False,
    )
```

profile of v0, /device:TPU:1, one launch (start us, length us, event | category | flops | bytes accessed | tf_op | source)
XLA Modules:
  0.0 377.9 jit_solution(12129984315452648051)
XLA Ops:
  0.7 1.2 copy-done
  1.9 1.3 convolution_bitcast_fusion.3
  3.4 4.4 %collective-permute-start = (f32[2,128]{1,0:T(2,128)S(1)}, f32[2,128]{1,0:T(2,128)S(1)}, u32[]{:S(2)}, u32[]{:S(2)}) collective-permute-start(f32[2,128]{1,0:T(2,128)S(1)} %fusion.94), channel_id=1, source_target_pairs={{0,1},{1,0},{2,3},{3,2},{4,5},{5,4},{6,7},{7,6},{8,9},{9,8},{10,11... | collective-permute-start | bytes 3080 | tf_op jit(solution)/shard_map/ppermute | solution.py:32
  7.7 0.9 collective-permute-done
  8.8 4.9 %collective-permute-start.1 = (f32[2,128]{1,0:T(2,128)S(1)}, f32[2,128]{1,0:T(2,128)S(1)}, u32[]{:S(2)}, u32[]{:S(2)}) collective-permute-start(f32[2,128]{1,0:T(2,128)S(1)} %fusion.86), channel_id=1, source_target_pairs={{0,2},{1,3},{2,0},{3,1},{4,6},{5,7},{6,4},{7,5},{8,10},{9,11},{10,... | collective-permute-start | bytes 3080 | tf_op jit(solution)/shard_map/ppermute | solution.py:32
  13.8 0.9 collective-permute-done.1
  14.9 8.8 %collective-permute-start.2 = (f32[2,128]{1,0:T(2,128)S(1)}, f32[2,128]{1,0:T(2,128)S(1)}, u32[]{:S(2)}, u32[]{:S(2)}) collective-permute-start(f32[2,128]{1,0:T(2,128)S(1)} %fusion.78), channel_id=1, source_target_pairs={{0,4},{1,5},{2,6},{3,7},{4,0},{5,1},{6,2},{7,3},{8,12},{9,13},{10,... | collective-permute-start | bytes 3080 | tf_op jit(solution)/shard_map/ppermute | solution.py:32
  23.7 0.9 collective-permute-done.2
  24.8 13.1 %collective-permute-start.3 = (f32[2,128]{1,0:T(2,128)S(1)}, f32[2,128]{1,0:T(2,128)S(1)}, u32[]{:S(2)}, u32[]{:S(2)}) collective-permute-start(f32[2,128]{1,0:T(2,128)S(1)} %fusion.70), channel_id=1, source_target_pairs={{0,8},{1,9},{2,10},{3,11},{4,12},{5,13},{6,14},{7,15},{8,0},{9,1},... | collective-permute-start | bytes 3080 | tf_op jit(solution)/shard_map/ppermute | solution.py:32
  37.9 0.9 collective-permute-done.3
  39.0 9.2 %collective-permute-start.4 = (f32[2,128]{1,0:T(2,128)S(1)}, f32[2,128]{1,0:T(2,128)S(1)}, u32[]{:S(2)}, u32[]{:S(2)}) collective-permute-start(f32[2,128]{1,0:T(2,128)S(1)} %fusion.62), channel_id=1, source_target_pairs={{0,16},{1,17},{2,18},{3,19},{4,20},{5,21},{6,22},{7,23},{8,24},{9,... | collective-permute-start | bytes 3080 | tf_op jit(solution)/shard_map/ppermute | solution.py:32
  48.2 0.8 collective-permute-done.4
  49.1 1.9 collective-permute-start.5
  51.1 2.4 collective-permute-done.5
  53.6 2.5 collective-permute-start.6
  56.2 3.3 collective-permute-done.6
  59.6 1.9 collective-permute-start.7
  61.5 0.8 reshape.70
  62.5 1.4 collective-permute-done.7
  64.1 2.5 collective-permute-start.8
  66.6 1.7 convolution_bitcast_fusion.1
  68.6 1.4 collective-permute-done.8
  73.5 0.5 copy-done.6
  74.2 1.0 convolution_add_fusion.1
  75.2 6.8 %collective-permute-start.10 = (f32[3,1,128]{2,0,1:T(4,128)S(1)}, f32[3,1,128]{2,0,1:T(4,128)S(1)}, u32[]{:S(2)}, u32[]{:S(2)}) collective-permute-start(f32[3,1,128]{2,0,1:T(4,128)S(1)} %get-tuple-element.18), channel_id=1, source_target_pairs={{16,0},{32,16},{48,32},{64,48},{80,64},{96,80},{112,96},{128,112},... | collective-permute-start | bytes 4616 | tf_op jit(solution)/shard_map/ppermute | solution.py:22
  82.0 1.9 collective-permute-start.9
  83.9 1.1 collective-permute-done.9
  85.2 1.6 collective-permute-start.11
  86.8 1.3 collective-permute-start.12
  88.1 3.4 collective-permute-done.12
  91.8 0.6 copy-done.5
  92.7 109.6 %all-reduce = (f32[2]{0:T(128)S(1)}, f32[2]{0:T(128)S(1)}) all-reduce(f32[2]{0:T(128)S(1)} %get-tuple-element.7, f32[2]{0:T(128)S(1)} %get-tuple-element.6), channel_id=1, replica_groups=mesh['gx'=32,'gy'=16] {'gx','gy'}, use_global_device_ids=true, to_apply=%region_1.0 | all-reduce | flops 4 | bytes 32 | tf_op jit(solution)/shard_map/psum | solution.py:119
  202.3 0.6 copy-done.18
  202.9 0.5 copy-done.16
  203.5 0.6 convolution_bitcast_fusion.2
  204.2 1.9 collective-permute-start.13
  206.2 2.4 collective-permute-done.13
  208.7 1.9 collective-permute-start.14
  210.6 3.3 collective-permute-done.14
  214.1 4.0 %collective-permute-start.15 = (f32[2,128]{1,0:T(2,128)S(1)}, f32[2,128]{1,0:T(2,128)S(1)}, u32[]{:S(2)}, u32[]{:S(2)}) collective-permute-start(f32[2,128]{1,0:T(2,128)S(1)} %fusion.74), channel_id=1, source_target_pairs={{0,4},{1,5},{2,6},{3,7},{4,0},{5,1},{6,2},{7,3},{8,12},{9,13},{10,... | collective-permute-start | bytes 3080 | tf_op jit(solution)/shard_map/ppermute | solution.py:32
  218.1 4.2 %collective-permute-done.15 = f32[2,128]{1,0:T(2,128)S(1)} collective-permute-done((f32[2,128]{1,0:T(2,128)S(1)}, f32[2,128]{1,0:T(2,128)S(1)}, u32[]{:S(2)}, u32[]{:S(2)}) %collective-permute-start.15) | collective-permute-done | bytes 1056 | tf_op jit(solution)/shard_map/ppermute | solution.py:32
  222.5 8.2 %collective-permute-start.16 = (f32[2,128]{1,0:T(2,128)S(1)}, f32[2,128]{1,0:T(2,128)S(1)}, u32[]{:S(2)}, u32[]{:S(2)}) collective-permute-start(f32[2,128]{1,0:T(2,128)S(1)} %fusion.66), channel_id=1, source_target_pairs={{0,8},{1,9},{2,10},{3,11},{4,12},{5,13},{6,14},{7,15},{8,0},{9,1},... | collective-permute-start | bytes 3080 | tf_op jit(solution)/shard_map/ppermute | solution.py:32
  230.7 4.8 %collective-permute-done.16 = f32[2,128]{1,0:T(2,128)S(1)} collective-permute-done((f32[2,128]{1,0:T(2,128)S(1)}, f32[2,128]{1,0:T(2,128)S(1)}, u32[]{:S(2)}, u32[]{:S(2)}) %collective-permute-start.16) | collective-permute-done | bytes 1056 | tf_op jit(solution)/shard_map/ppermute | solution.py:32
  236.0 7.7 %collective-permute-start.17 = (f32[2,128]{1,0:T(2,128)S(1)}, f32[2,128]{1,0:T(2,128)S(1)}, u32[]{:S(2)}, u32[]{:S(2)}) collective-permute-start(f32[2,128]{1,0:T(2,128)S(1)} %fusion.58), channel_id=1, source_target_pairs={{0,16},{1,17},{2,18},{3,19},{4,20},{5,21},{6,22},{7,23},{8,24},{9,... | collective-permute-start | bytes 3080 | tf_op jit(solution)/shard_map/ppermute | solution.py:32
  243.7 0.8 collective-permute-done.17
  245.1 1.9 collective-permute-start.18
  247.0 2.4 collective-permute-done.18
  250.0 2.5 collective-permute-start.19
  252.5 3.3 collective-permute-done.19
  256.3 1.9 collective-permute-start.20
  258.5 2.2 collective-permute-done.20
  260.7 0.8 fusion.26
  261.6 2.8 collective-permute-start.21
  264.3 1.7 convolution_bitcast_fusion
  266.1 0.6 copy.19
  267.7 0.9 convolution_add_fusion.10
  268.8 0.5 copy-done.15
  269.6 0.5 copy-done.13
  270.5 0.5 copy-done.11
  273.5 1.1 multiply_reduce_fusion
  274.6 101.4 %psum.23 = f32[2]{0:T(128)S(1)} all-reduce(f32[2]{0:T(128)S(1)} %get-tuple-element.21), channel_id=1, replica_groups=mesh['gx'=32,'gy'=16] {'gx','gy'}, use_global_device_ids=true, to_apply=%region_5.0 | all-reduce | flops 2 | bytes 16 | tf_op jit(solution)/shard_map/psum | solution.py:126
  376.0 0.6 copy-done.17
  376.7 0.6 copy.18
  377.3 0.6 copy.20
  (110 shorter events, 13.7 us)
Async XLA Ops:
  0.6 1.2 copy-start
  0.6 2.5 copy-start.4
  0.7 8.0 %copy-start.1 = (f32[1,1,8,128,128]{4,3,2,1,0:T(8,128)S(1)}, f32[1,1,8,128,128]{4,3,2,1,0:T(8,128)}, u32[]{:S(2)}) copy-start(f32[1,1,8,128,128]{4,3,2,1,0:T(8,128)} %param.13) | copy-start | bytes 1572868
  0.7 65.9 %copy-start.2 = (f32[4,4,128,128]{3,2,1,0:T(8,128)S(1)}, f32[4,4,128,128]{3,2,1,0:T(8,128)}, u32[]{:S(2)}) copy-start(f32[4,4,128,128]{3,2,1,0:T(8,128)} %param.10) | copy-start | bytes 3145732
  3.4 5.3 %collective-permute-start = (f32[2,128]{1,0:T(2,128)S(1)}, f32[2,128]{1,0:T(2,128)S(1)}, u32[]{:S(2)}, u32[]{:S(2)}) collective-permute-start(f32[2,128]{1,0:T(2,128)S(1)} %fusion.94), channel_id=1, source_target_pairs={{0,1},{1,0},{2,3},{3,2},{4,5},{5,4},{6,7},{7,6},{8,9},{9,8},{10,11... | collective-permute-start | bytes 3080 | tf_op jit(solution)/shard_map/ppermute | solution.py:32
  8.8 5.9 %collective-permute-start.1 = (f32[2,128]{1,0:T(2,128)S(1)}, f32[2,128]{1,0:T(2,128)S(1)}, u32[]{:S(2)}, u32[]{:S(2)}) collective-permute-start(f32[2,128]{1,0:T(2,128)S(1)} %fusion.86), channel_id=1, source_target_pairs={{0,2},{1,3},{2,0},{3,1},{4,6},{5,7},{6,4},{7,5},{8,10},{9,11},{10,... | collective-permute-start | bytes 3080 | tf_op jit(solution)/shard_map/ppermute | solution.py:32
  14.9 9.8 %collective-permute-start.2 = (f32[2,128]{1,0:T(2,128)S(1)}, f32[2,128]{1,0:T(2,128)S(1)}, u32[]{:S(2)}, u32[]{:S(2)}) collective-permute-start(f32[2,128]{1,0:T(2,128)S(1)} %fusion.78), channel_id=1, source_target_pairs={{0,4},{1,5},{2,6},{3,7},{4,0},{5,1},{6,2},{7,3},{8,12},{9,13},{10,... | collective-permute-start | bytes 3080 | tf_op jit(solution)/shard_map/ppermute | solution.py:32
  24.8 14.0 %collective-permute-start.3 = (f32[2,128]{1,0:T(2,128)S(1)}, f32[2,128]{1,0:T(2,128)S(1)}, u32[]{:S(2)}, u32[]{:S(2)}) collective-permute-start(f32[2,128]{1,0:T(2,128)S(1)} %fusion.70), channel_id=1, source_target_pairs={{0,8},{1,9},{2,10},{3,11},{4,12},{5,13},{6,14},{7,15},{8,0},{9,1},... | collective-permute-start | bytes 3080 | tf_op jit(solution)/shard_map/ppermute | solution.py:32
  39.0 10.0 %collective-permute-start.4 = (f32[2,128]{1,0:T(2,128)S(1)}, f32[2,128]{1,0:T(2,128)S(1)}, u32[]{:S(2)}, u32[]{:S(2)}) collective-permute-start(f32[2,128]{1,0:T(2,128)S(1)} %fusion.62), channel_id=1, source_target_pairs={{0,16},{1,17},{2,18},{3,19},{4,20},{5,21},{6,22},{7,23},{8,24},{9,... | collective-permute-start | bytes 3080 | tf_op jit(solution)/shard_map/ppermute | solution.py:32
  49.1 4.3 %collective-permute-start.5 = (f32[2,128]{1,0:T(2,128)S(1)}, f32[2,128]{1,0:T(2,128)S(1)}, u32[]{:S(2)}, u32[]{:S(2)}) collective-permute-start(f32[2,128]{1,0:T(2,128)S(1)} %fusion.54), channel_id=1, source_target_pairs={{0,32},{1,33},{2,34},{3,35},{4,36},{5,37},{6,38},{7,39},{8,40},{9,... | collective-permute-start | bytes 3080 | tf_op jit(solution)/shard_map/ppermute | solution.py:32
  53.6 5.8 %collective-permute-start.6 = (f32[2,128]{1,0:T(2,128)S(1)}, f32[2,128]{1,0:T(2,128)S(1)}, u32[]{:S(2)}, u32[]{:S(2)}) collective-permute-start(f32[2,128]{1,0:T(2,128)S(1)} %fusion.46), channel_id=1, source_target_pairs={{0,64},{1,65},{2,66},{3,67},{4,68},{5,69},{6,70},{7,71},{8,72},{9,... | collective-permute-start | bytes 3080 | tf_op jit(solution)/shard_map/ppermute | solution.py:32
  59.6 4.3 %collective-permute-start.7 = (f32[2,128]{1,0:T(2,128)S(1)}, f32[2,128]{1,0:T(2,128)S(1)}, u32[]{:S(2)}, u32[]{:S(2)}) collective-permute-start(f32[2,128]{1,0:T(2,128)S(1)} %fusion.38), channel_id=1, source_target_pairs={{0,128},{1,129},{2,130},{3,131},{4,132},{5,133},{6,134},{7,135},{8... | collective-permute-start | bytes 3080 | tf_op jit(solution)/shard_map/ppermute | solution.py:32
  64.1 6.0 %copy-start.3 = (f32[1,1,9,128,128]{4,3,2,1,0:T(8,128)S(1)}, f32[1,1,9,128,128]{4,3,2,1,0:T(8,128)}, u32[]{:S(2)}) copy-start(f32[1,1,9,128,128]{4,3,2,1,0:T(8,128)} %param.15) | copy-start | bytes 1769476
  64.1 6.0 %collective-permute-start.8 = (f32[2,128]{1,0:T(2,128)S(1)}, f32[2,128]{1,0:T(2,128)S(1)}, u32[]{:S(2)}, u32[]{:S(2)}) collective-permute-start(f32[2,128]{1,0:T(2,128)S(1)} %fusion.30), channel_id=1, source_target_pairs={{0,256},{1,257},{2,258},{3,259},{4,260},{5,261},{6,262},{7,263},{8... | collective-permute-start | bytes 3080 | tf_op jit(solution)/shard_map/ppermute | solution.py:32
  73.1 0.9 copy-start.6
  74.2 1.0 copy-start.7
  75.2 8.8 %collective-permute-start.10 = (f32[3,1,128]{2,0,1:T(4,128)S(1)}, f32[3,1,128]{2,0,1:T(4,128)S(1)}, u32[]{:S(2)}, u32[]{:S(2)}) collective-permute-start(f32[3,1,128]{2,0,1:T(4,128)S(1)} %get-tuple-element.18), channel_id=1, source_target_pairs={{16,0},{32,16},{48,32},{64,48},{80,64},{96,80},{112,96},{128,112},... | collective-permute-start | bytes 4616 | tf_op jit(solution)/shard_map/ppermute | solution.py:22
  82.0 3.1 collective-permute-start.9
  85.2 3.0 collective-permute-start.11
  86.8 4.7 %collective-permute-start.12 = (f32[3,18,1]{2,0,1:T(4,128)S(1)}, f32[3,18,1]{2,0,1:T(4,128)S(1)}, u32[]{:S(2)}, u32[]{:S(2)}) collective-permute-start(f32[3,18,1]{2,0,1:T(4,128)S(1)} %get-tuple-element.11), channel_id=1, source_target_pairs={{1,0},{2,1},{3,2},{4,3},{5,4},{6,5},{7,6},{8,7},{9,8},{10,9},{11,1... | collective-permute-start | bytes 656 | tf_op jit(solution)/shard_map/ppermute | solution.py:22
  91.7 0.7 copy-start.5
  202.3 0.6 copy-start.18
  202.9 0.5 copy-start.16
  204.2 4.3 %collective-permute-start.13 = (f32[2,128]{1,0:T(2,128)S(1)}, f32[2,128]{1,0:T(2,128)S(1)}, u32[]{:S(2)}, u32[]{:S(2)}) collective-permute-start(f32[2,128]{1,0:T(2,128)S(1)} %fusion.90), channel_id=1, source_target_pairs={{0,1},{1,0},{2,3},{3,2},{4,5},{5,4},{6,7},{7,6},{8,9},{9,8},{10,11... | collective-permute-start | bytes 3080 | tf_op jit(solution)/shard_map/ppermute | solution.py:32
  208.7 5.2 %collective-permute-start.14 = (f32[2,128]{1,0:T(2,128)S(1)}, f32[2,128]{1,0:T(2,128)S(1)}, u32[]{:S(2)}, u32[]{:S(2)}) collective-permute-start(f32[2,128]{1,0:T(2,128)S(1)} %fusion.82), channel_id=1, source_target_pairs={{0,2},{1,3},{2,0},{3,1},{4,6},{5,7},{6,4},{7,5},{8,10},{9,11},{10,... | collective-permute-start | bytes 3080 | tf_op jit(solution)/shard_map/ppermute | solution.py:32
  214.1 8.2 %collective-permute-start.15 = (f32[2,128]{1,0:T(2,128)S(1)}, f32[2,128]{1,0:T(2,128)S(1)}, u32[]{:S(2)}, u32[]{:S(2)}) collective-permute-start(f32[2,128]{1,0:T(2,128)S(1)} %fusion.74), channel_id=1, source_target_pairs={{0,4},{1,5},{2,6},{3,7},{4,0},{5,1},{6,2},{7,3},{8,12},{9,13},{10,... | collective-permute-start | bytes 3080 | tf_op jit(solution)/shard_map/ppermute | solution.py:32
  222.5 13.0 %collective-permute-start.16 = (f32[2,128]{1,0:T(2,128)S(1)}, f32[2,128]{1,0:T(2,128)S(1)}, u32[]{:S(2)}, u32[]{:S(2)}) collective-permute-start(f32[2,128]{1,0:T(2,128)S(1)} %fusion.66), channel_id=1, source_target_pairs={{0,8},{1,9},{2,10},{3,11},{4,12},{5,13},{6,14},{7,15},{8,0},{9,1},... | collective-permute-start | bytes 3080 | tf_op jit(solution)/shard_map/ppermute | solution.py:32
  235.5 0.5 copy-start.8
  236.0 8.5 %collective-permute-start.17 = (f32[2,128]{1,0:T(2,128)S(1)}, f32[2,128]{1,0:T(2,128)S(1)}, u32[]{:S(2)}, u32[]{:S(2)}) collective-permute-start(f32[2,128]{1,0:T(2,128)S(1)} %fusion.58), channel_id=1, source_target_pairs={{0,16},{1,17},{2,18},{3,19},{4,20},{5,21},{6,22},{7,23},{8,24},{9,... | collective-permute-start | bytes 3080 | tf_op jit(solution)/shard_map/ppermute | solution.py:32
  244.5 0.6 copy-start.10
  245.1 4.3 %collective-permute-start.18 = (f32[2,128]{1,0:T(2,128)S(1)}, f32[2,128]{1,0:T(2,128)S(1)}, u32[]{:S(2)}, u32[]{:S(2)}) collective-permute-start(f32[2,128]{1,0:T(2,128)S(1)} %fusion.50), channel_id=1, source_target_pairs={{0,32},{1,33},{2,34},{3,35},{4,36},{5,37},{6,38},{7,39},{8,40},{9,... | collective-permute-start | bytes 3080 | tf_op jit(solution)/shard_map/ppermute | solution.py:32
  249.4 0.6 copy-start.12
  250.0 5.8 %collective-permute-start.19 = (f32[2,128]{1,0:T(2,128)S(1)}, f32[2,128]{1,0:T(2,128)S(1)}, u32[]{:S(2)}, u32[]{:S(2)}) collective-permute-start(f32[2,128]{1,0:T(2,128)S(1)} %fusion.42), channel_id=1, source_target_pairs={{0,64},{1,65},{2,66},{3,67},{4,68},{5,69},{6,70},{7,71},{8,72},{9,... | collective-permute-start | bytes 3080 | tf_op jit(solution)/shard_map/ppermute | solution.py:32
  255.8 0.6 copy-start.14
  256.3 4.4 %collective-permute-start.20 = (f32[2,128]{1,0:T(2,128)S(1)}, f32[2,128]{1,0:T(2,128)}, u32[]{:S(2)}, u32[]{:S(2)}) collective-permute-start(f32[2,128]{1,0:T(2,128)S(1)} %fusion.34), channel_id=1, source_target_pairs={{0,128},{1,129},{2,130},{3,131},{4,132},{5,133},{6,134},{7,135},{8... | collective-permute-start | bytes 3080 | tf_op jit(solution)/shard_map/ppermute | solution.py:32
  261.6 5.8 %collective-permute-start.21 = (f32[2,128]{1,0:T(2,128)S(1)}, f32[2,128]{1,0:T(2,128)S(1)}, u32[]{:S(2)}, u32[]{:S(2)}) collective-permute-start(f32[2,128]{1,0:T(2,128)S(1)} %fusion.26), channel_id=1, source_target_pairs={{0,256},{1,257},{2,258},{3,259},{4,260},{5,261},{6,262},{7,263},{8... | collective-permute-start | bytes 3080 | tf_op jit(solution)/shard_map/ppermute | solution.py:32
  268.6 0.7 copy-start.15
  269.4 0.7 copy-start.13
  270.3 0.7 copy-start.11
  271.1 0.7 copy-start.9
  274.6 101.4 %copy-start.19 = (f32[2]{0:T(128)S(1)}, f32[2]{0:T(128)}, u32[]{:S(2)}) copy-start(f32[2]{0:T(128)} %copy-done.18) | copy-start | bytes 28
  376.0 0.6 copy-start.17
where the time goes:
time: 379 us; the launch traced here: 378 us
  blocking collectives  211 us (56%)
  starting transfers between devices  93.8 us (25%)
  waiting for transfers between devices  41.5 us (11%)
  matrix products  18.7 us (5%)
  local copies, waits for them, and re-layouts  11.2 us (3%)
    psum x1, blocking collectives, on_device(): rz_old = lax.psum(local_rz, ('gx', 'gy'))  110 us
    psum x1, blocking collectives, on_device(): rz_new = lax.psum(jnp.sum(residual * second_z, axis=(1, 2)), ('gx', 'gy'))  101 us
    ppermute x18, starting transfers between devices, from_partner(): return lax.ppermute(value, axis, pairs)  82.1 us
    ppermute x18, waiting for transfers between devices, from_partner(): return lax.ppermute(value, axis, pairs)  37 us
    unnamed x44, local copies, waits for them, and re-layouts  9.48 us
    ppermute x2, starting transfers between devices, extended(): lax.ppermute(head, axis, [((i + 1) % count, i) for i in range(ends)])  8.12 us
  transfers between devices with their start and end apart: 22, of which 20 were waited for; matrix products, arithmetic and copies ran while one was open for 2% of the time, Pallas kernels for 0%

commit v1 on v0

--- a/solution.py
+++ b/solution.py
@@ -116,7 +116,7 @@
     )
     first_z = apply_inverse(right_side)
     local_rz = jnp.sum(right_side * first_z, axis=(1, 2))
-    rz_old = lax.psum(local_rz, ("gx", "gy"))
+    rz_old = lax.psum(lax.psum(local_rz, "gx"), "gy")
     applied = stencil(first_z, conductivity)
     curvature = lax.psum(jnp.sum(first_z * applied, axis=(1, 2)), ("gx", "gy"))
     step_size = (rz_old / curvature)[:, None, None]

time: 379 us -> 470 us (1.24)
  blocking collectives: 211 us -> 301 us
  starting transfers between devices: 93.8 us -> 104 us
  waiting for transfers between devices: 41.5 us -> 31.9 us
    psum x1 -> x3, blocking collectives: 110 us -> 197 us  [the longest x1 106 us: on_device(): curvature = lax.psum(jnp.sum(first_z * applied, axis=(1, 2)), ('gx', 'gy'))]
    ppermute x18, starting transfers between devices: 82.1 us -> 92.4 us  [from_partner(): return lax.ppermute(value, axis, pairs)]
    ppermute x18, waiting for transfers between devices: 37 us -> 27.4 us  [from_partner(): return lax.ppermute(value, axis, pairs)]
  transfers between devices with their start and end apart: 22 -> 22, of which waited for: 20 -> 19; matrix products, arithmetic and copies ran while one was open for 2% -> 1% of each run, Pallas kernels for 0% -> 0%
where the time goes in v1:
time: 470 us; the launch traced here: 469 us
  blocking collectives  301 us (64%)
  starting transfers between devices  104 us (22%)
  waiting for transfers between devices  31.9 us (7%)
  matrix products  18.6 us (4%)
  local copies, waits for them, and re-layouts  10.9 us (2%)
    psum x1, blocking collectives, on_device(): curvature = lax.psum(jnp.sum(first_z * applied, axis=(1, 2)), ('gx', 'gy'))  106 us
    psum x1, blocking collectives, on_device(): rz_new = lax.psum(jnp.sum(residual * second_z, axis=(1, 2)), ('gx', 'gy'))  105 us
    ppermute x18, starting transfers between devices, from_partner(): return lax.ppermute(value, axis, pairs)  92.4 us
    psum x2, blocking collectives, on_device(): rz_old = lax.psum(lax.psum(local_rz, 'gx'), 'gy')  90.7 us
    ppermute x18, waiting for transfers between devices, from_partner(): return lax.ppermute(value, axis, pairs)  27.4 us
  transfers between devices with their start and end apart: 22, of which 19 were waited for; matrix products, arithmetic and copies ran while one was open for 1% of the time, Pallas kernels for 0%

profile of v1, /device:TPU:1, one launch (start us, length us, event | category | flops | bytes accessed | tf_op | source)
XLA Modules:
  0.0 468.6 jit_solution(5560506469664577124)
XLA Ops:
  0.7 1.2 copy-done
  1.9 1.3 convolution_bitcast_fusion.3
  3.4 4.4 collective-permute-start
  7.7 0.9 collective-permute-done
  8.8 4.9 %collective-permute-start.1 = (f32[2,128]{1,0:T(2,128)S(1)}, f32[2,128]{1,0:T(2,128)S(1)}, u32[]{:S(2)}, u32[]{:S(2)}) collective-permute-start(f32[2,128]{1,0:T(2,128)S(1)} %fusion.86), channel_id=1, source_target_pairs={{0,2},{1,3},{2,0},{3,1},{4,6},{5,7},{6,4},{7,5},{8,10},{9,11},{10,... | collective-permute-start | bytes 3080 | tf_op jit(solution)/shard_map/ppermute | solution.py:32
  13.8 0.9 collective-permute-done.1
  14.9 8.8 %collective-permute-start.2 = (f32[2,128]{1,0:T(2,128)S(1)}, f32[2,128]{1,0:T(2,128)S(1)}, u32[]{:S(2)}, u32[]{:S(2)}) collective-permute-start(f32[2,128]{1,0:T(2,128)S(1)} %fusion.78), channel_id=1, source_target_pairs={{0,4},{1,5},{2,6},{3,7},{4,0},{5,1},{6,2},{7,3},{8,12},{9,13},{10,... | collective-permute-start | bytes 3080 | tf_op jit(solution)/shard_map/ppermute | solution.py:32
  23.7 0.9 collective-permute-done.2
  24.8 13.1 %collective-permute-start.3 = (f32[2,128]{1,0:T(2,128)S(1)}, f32[2,128]{1,0:T(2,128)S(1)}, u32[]{:S(2)}, u32[]{:S(2)}) collective-permute-start(f32[2,128]{1,0:T(2,128)S(1)} %fusion.70), channel_id=1, source_target_pairs={{0,8},{1,9},{2,10},{3,11},{4,12},{5,13},{6,14},{7,15},{8,0},{9,1},... | collective-permute-start | bytes 3080 | tf_op jit(solution)/shard_map/ppermute | solution.py:32
  37.9 0.9 collective-permute-done.3
  39.0 9.2 %collective-permute-start.4 = (f32[2,128]{1,0:T(2,128)S(1)}, f32[2,128]{1,0:T(2,128)S(1)}, u32[]{:S(2)}, u32[]{:S(2)}) collective-permute-start(f32[2,128]{1,0:T(2,128)S(1)} %fusion.62), channel_id=1, source_target_pairs={{0,16},{1,17},{2,18},{3,19},{4,20},{5,21},{6,22},{7,23},{8,24},{9,... | collective-permute-start | bytes 3080 | tf_op jit(solution)/shard_map/ppermute | solution.py:32
  48.2 0.8 collective-permute-done.4
  49.1 1.9 collective-permute-start.5
  51.1 2.4 collective-permute-done.5
  53.6 2.5 collective-permute-start.6
  56.2 3.3 collective-permute-done.6
  59.6 1.9 collective-permute-start.7
  61.5 0.8 reshape.70
  62.5 1.4 collective-permute-done.7
  64.1 2.5 collective-permute-start.8
  66.6 1.7 convolution_bitcast_fusion.1
  68.6 1.4 collective-permute-done.8
  74.2 1.0 convolution_add_fusion.1
  75.2 6.8 %collective-permute-start.10 = (f32[3,1,128]{2,0,1:T(4,128)S(1)}, f32[3,1,128]{2,0,1:T(4,128)S(1)}, u32[]{:S(2)}, u32[]{:S(2)}) collective-permute-start(f32[3,1,128]{2,0,1:T(4,128)S(1)} %get-tuple-element.16), channel_id=1, source_target_pairs={{16,0},{32,16},{48,32},{64,48},{80,64},{96,80},{112,96},{128,112},... | collective-permute-start | bytes 4616 | tf_op jit(solution)/shard_map/ppermute | solution.py:22
  82.0 1.9 collective-permute-start.9
  83.9 1.1 collective-permute-done.9
  85.2 1.6 collective-permute-start.11
  86.8 1.3 collective-permute-start.12
  88.1 3.4 collective-permute-done.12
  91.8 0.6 copy-done.5
  92.7 64.3 %psum.28 = f32[2]{0:T(128)S(1)} all-reduce(f32[2]{0:T(128)S(1)} %get-tuple-element.7), channel_id=1, replica_groups=mesh['gx'=32,'gy'=16] {'gx'}, use_global_device_ids=true, to_apply=%region_1.0 | all-reduce | flops 2 | bytes 16 | tf_op jit(solution)/shard_map/psum | solution.py:119
  157.0 26.4 %psum.29 = f32[2]{0:T(128)S(1)} all-reduce(f32[2]{0:T(128)S(1)} %psum.28), channel_id=1, replica_groups=mesh['gx'=32,'gy'=16] {'gy'}, use_global_device_ids=true, to_apply=%region_2.0 | all-reduce | flops 2 | bytes 16 | tf_op jit(solution)/shard_map/psum | solution.py:119
  183.4 105.9 %psum.30 = f32[2]{0:T(128)S(1)} all-reduce(f32[2]{0:T(128)S(1)} %get-tuple-element.6), channel_id=1, replica_groups=mesh['gx'=32,'gy'=16] {'gx','gy'}, use_global_device_ids=true, to_apply=%region_4.0 | all-reduce | flops 2 | bytes 16 | tf_op jit(solution)/shard_map/psum | solution.py:121
  289.3 0.6 copy-done.16
  290.0 0.6 convolution_bitcast_fusion.2
  290.7 3.7 collective-permute-start.13
  294.5 0.9 collective-permute-done.13
  295.6 3.0 collective-permute-start.14
  298.6 2.2 collective-permute-done.14
  300.9 5.2 %collective-permute-start.15 = (f32[2,128]{1,0:T(2,128)S(1)}, f32[2,128]{1,0:T(2,128)S(1)}, u32[]{:S(2)}, u32[]{:S(2)}) collective-permute-start(f32[2,128]{1,0:T(2,128)S(1)} %fusion.74), channel_id=1, source_target_pairs={{0,4},{1,5},{2,6},{3,7},{4,0},{5,1},{6,2},{7,3},{8,12},{9,13},{10,... | collective-permute-start | bytes 3080 | tf_op jit(solution)/shard_map/ppermute | solution.py:32
  306.1 3.1 collective-permute-done.15
  309.3 9.3 %collective-permute-start.16 = (f32[2,128]{1,0:T(2,128)S(1)}, f32[2,128]{1,0:T(2,128)S(1)}, u32[]{:S(2)}, u32[]{:S(2)}) collective-permute-start(f32[2,128]{1,0:T(2,128)S(1)} %fusion.66), channel_id=1, source_target_pairs={{0,8},{1,9},{2,10},{3,11},{4,12},{5,13},{6,14},{7,15},{8,0},{9,1},... | collective-permute-start | bytes 3080 | tf_op jit(solution)/shard_map/ppermute | solution.py:32
  318.7 3.7 collective-permute-done.16
  322.9 6.9 %collective-permute-start.17 = (f32[2,128]{1,0:T(2,128)S(1)}, f32[2,128]{1,0:T(2,128)S(1)}, u32[]{:S(2)}, u32[]{:S(2)}) collective-permute-start(f32[2,128]{1,0:T(2,128)S(1)} %fusion.58), channel_id=1, source_target_pairs={{0,16},{1,17},{2,18},{3,19},{4,20},{5,21},{6,22},{7,23},{8,24},{9,... | collective-permute-start | bytes 3080 | tf_op jit(solution)/shard_map/ppermute | solution.py:32
  329.8 0.8 collective-permute-done.17
  331.2 3.2 collective-permute-start.18
  334.4 1.1 collective-permute-done.18
  336.1 4.2 collective-permute-start.19
  340.3 1.6 collective-permute-done.19
  342.4 3.2 collective-permute-start.20
  345.9 0.9 collective-permute-done.20
  346.8 0.8 fusion.26
  347.6 4.4 collective-permute-start.21
  352.0 1.7 convolution_bitcast_fusion
  353.8 0.6 copy.19
  355.0 0.9 convolution_add_fusion.10
  356.0 0.5 copy-done.15
  356.9 0.5 copy-done.13
  357.7 0.5 copy-done.11
  360.8 1.1 multiply_reduce_fusion
  361.9 104.7 %psum.31 = f32[2]{0:T(128)S(1)} all-reduce(f32[2]{0:T(128)S(1)} %get-tuple-element.19), channel_id=1, replica_groups=mesh['gx'=32,'gy'=16] {'gx','gy'}, use_global_device_ids=true, to_apply=%region_6.0 | all-reduce | flops 2 | bytes 16 | tf_op jit(solution)/shard_map/psum | solution.py:126
  466.6 0.7 copy-done.17
  467.4 0.6 copy.18
  468.0 0.6 copy.20
  (112 shorter events, 13.9 us)
Async XLA Ops:
  0.6 1.2 copy-start
  0.6 2.5 copy-start.4
  0.7 8.0 %copy-start.1 = (f32[1,1,8,128,128]{4,3,2,1,0:T(8,128)S(1)}, f32[1,1,8,128,128]{4,3,2,1,0:T(8,128)}, u32[]{:S(2)}) copy-start(f32[1,1,8,128,128]{4,3,2,1,0:T(8,128)} %param.13) | copy-start | bytes 1572868
  0.7 65.9 %copy-start.2 = (f32[4,4,128,128]{3,2,1,0:T(8,128)S(1)}, f32[4,4,128,128]{3,2,1,0:T(8,128)}, u32[]{:S(2)}) copy-start(f32[4,4,128,128]{3,2,1,0:T(8,128)} %param.10) | copy-start | bytes 3145732
  3.4 5.3 %collective-permute-start = (f32[2,128]{1,0:T(2,128)S(1)}, f32[2,128]{1,0:T(2,128)S(1)}, u32[]{:S(2)}, u32[]{:S(2)}) collective-permute-start(f32[2,128]{1,0:T(2,128)S(1)} %fusion.94), channel_id=1, source_target_pairs={{0,1},{1,0},{2,3},{3,2},{4,5},{5,4},{6,7},{7,6},{8,9},{9,8},{10,11... | collective-permute-start | bytes 3080 | tf_op jit(solution)/shard_map/ppermute | solution.py:32
  8.8 5.9 %collective-permute-start.1 = (f32[2,128]{1,0:T(2,128)S(1)}, f32[2,128]{1,0:T(2,128)S(1)}, u32[]{:S(2)}, u32[]{:S(2)}) collective-permute-start(f32[2,128]{1,0:T(2,128)S(1)} %fusion.86), channel_id=1, source_target_pairs={{0,2},{1,3},{2,0},{3,1},{4,6},{5,7},{6,4},{7,5},{8,10},{9,11},{10,... | collective-permute-start | bytes 3080 | tf_op jit(solution)/shard_map/ppermute | solution.py:32
  14.9 9.8 %collective-permute-start.2 = (f32[2,128]{1,0:T(2,128)S(1)}, f32[2,128]{1,0:T(2,128)S(1)}, u32[]{:S(2)}, u32[]{:S(2)}) collective-permute-start(f32[2,128]{1,0:T(2,128)S(1)} %fusion.78), channel_id=1, source_target_pairs={{0,4},{1,5},{2,6},{3,7},{4,0},{5,1},{6,2},{7,3},{8,12},{9,13},{10,... | collective-permute-start | bytes 3080 | tf_op jit(solution)/shard_map/ppermute | solution.py:32
  24.8 14.0 %collective-permute-start.3 = (f32[2,128]{1,0:T(2,128)S(1)}, f32[2,128]{1,0:T(2,128)S(1)}, u32[]{:S(2)}, u32[]{:S(2)}) collective-permute-start(f32[2,128]{1,0:T(2,128)S(1)} %fusion.70), channel_id=1, source_target_pairs={{0,8},{1,9},{2,10},{3,11},{4,12},{5,13},{6,14},{7,15},{8,0},{9,1},... | collective-permute-start | bytes 3080 | tf_op jit(solution)/shard_map/ppermute | solution.py:32
  39.0 10.0 %collective-permute-start.4 = (f32[2,128]{1,0:T(2,128)S(1)}, f32[2,128]{1,0:T(2,128)S(1)}, u32[]{:S(2)}, u32[]{:S(2)}) collective-permute-start(f32[2,128]{1,0:T(2,128)S(1)} %fusion.62), channel_id=1, source_target_pairs={{0,16},{1,17},{2,18},{3,19},{4,20},{5,21},{6,22},{7,23},{8,24},{9,... | collective-permute-start | bytes 3080 | tf_op jit(solution)/shard_map/ppermute | solution.py:32
  49.1 4.3 collective-permute-start.5
  53.6 5.8 %collective-permute-start.6 = (f32[2,128]{1,0:T(2,128)S(1)}, f32[2,128]{1,0:T(2,128)S(1)}, u32[]{:S(2)}, u32[]{:S(2)}) collective-permute-start(f32[2,128]{1,0:T(2,128)S(1)} %fusion.46), channel_id=1, source_target_pairs={{0,64},{1,65},{2,66},{3,67},{4,68},{5,69},{6,70},{7,71},{8,72},{9,... | collective-permute-start | bytes 3080 | tf_op jit(solution)/shard_map/ppermute | solution.py:32
  59.6 4.3 collective-permute-start.7
  64.1 6.0 %copy-start.3 = (f32[1,1,9,128,128]{4,3,2,1,0:T(8,128)S(1)}, f32[1,1,9,128,128]{4,3,2,1,0:T(8,128)}, u32[]{:S(2)}) copy-start(f32[1,1,9,128,128]{4,3,2,1,0:T(8,128)} %param.15) | copy-start | bytes 1769476
  64.1 6.0 %collective-permute-start.8 = (f32[2,128]{1,0:T(2,128)S(1)}, f32[2,128]{1,0:T(2,128)S(1)}, u32[]{:S(2)}, u32[]{:S(2)}) collective-permute-start(f32[2,128]{1,0:T(2,128)S(1)} %fusion.30), channel_id=1, source_target_pairs={{0,256},{1,257},{2,258},{3,259},{4,260},{5,261},{6,262},{7,263},{8... | collective-permute-start | bytes 3080 | tf_op jit(solution)/shard_map/ppermute | solution.py:32
  73.1 0.9 copy-start.6
  74.2 1.0 copy-start.7
  75.2 8.8 %collective-permute-start.10 = (f32[3,1,128]{2,0,1:T(4,128)S(1)}, f32[3,1,128]{2,0,1:T(4,128)S(1)}, u32[]{:S(2)}, u32[]{:S(2)}) collective-permute-start(f32[3,1,128]{2,0,1:T(4,128)S(1)} %get-tuple-element.16), channel_id=1, source_target_pairs={{16,0},{32,16},{48,32},{64,48},{80,64},{96,80},{112,96},{128,112},... | collective-permute-start | bytes 4616 | tf_op jit(solution)/shard_map/ppermute | solution.py:22
  82.0 3.1 collective-permute-start.9
  85.2 3.0 collective-permute-start.11
  86.8 4.7 %collective-permute-start.12 = (f32[3,18,1]{2,0,1:T(4,128)S(1)}, f32[3,18,1]{2,0,1:T(4,128)S(1)}, u32[]{:S(2)}, u32[]{:S(2)}) collective-permute-start(f32[3,18,1]{2,0,1:T(4,128)S(1)} %get-tuple-element.9), channel_id=1, source_target_pairs={{1,0},{2,1},{3,2},{4,3},{5,4},{6,5},{7,6},{8,7},{9,8},{10,9},{11,1... | collective-permute-start | bytes 656 | tf_op jit(solution)/shard_map/ppermute | solution.py:22
  91.7 0.7 copy-start.5
  183.4 105.9 %copy-start.18 = (f32[2]{0:T(128)}, f32[2]{0:T(128)S(1)}, u32[]{:S(2)}) copy-start(f32[2]{0:T(128)S(1)} %psum.29) | copy-start | bytes 28
  289.3 0.6 copy-start.16
  290.7 4.6 collective-permute-start.13
  295.6 5.2 %collective-permute-start.14 = (f32[2,128]{1,0:T(2,128)S(1)}, f32[2,128]{1,0:T(2,128)S(1)}, u32[]{:S(2)}, u32[]{:S(2)}) collective-permute-start(f32[2,128]{1,0:T(2,128)S(1)} %fusion.82), channel_id=1, source_target_pairs={{0,2},{1,3},{2,0},{3,1},{4,6},{5,7},{6,4},{7,5},{8,10},{9,11},{10,... | collective-permute-start | bytes 3080 | tf_op jit(solution)/shard_map/ppermute | solution.py:32
  300.9 8.2 %collective-permute-start.15 = (f32[2,128]{1,0:T(2,128)S(1)}, f32[2,128]{1,0:T(2,128)S(1)}, u32[]{:S(2)}, u32[]{:S(2)}) collective-permute-start(f32[2,128]{1,0:T(2,128)S(1)} %fusion.74), channel_id=1, source_target_pairs={{0,4},{1,5},{2,6},{3,7},{4,0},{5,1},{6,2},{7,3},{8,12},{9,13},{10,... | collective-permute-start | bytes 3080 | tf_op jit(solution)/shard_map/ppermute | solution.py:32
  309.3 13.0 %collective-permute-start.16 = (f32[2,128]{1,0:T(2,128)S(1)}, f32[2,128]{1,0:T(2,128)S(1)}, u32[]{:S(2)}, u32[]{:S(2)}) collective-permute-start(f32[2,128]{1,0:T(2,128)S(1)} %fusion.66), channel_id=1, source_target_pairs={{0,8},{1,9},{2,10},{3,11},{4,12},{5,13},{6,14},{7,15},{8,0},{9,1},... | collective-permute-start | bytes 3080 | tf_op jit(solution)/shard_map/ppermute | solution.py:32
  322.3 0.6 copy-start.8
  322.9 7.7 %collective-permute-start.17 = (f32[2,128]{1,0:T(2,128)S(1)}, f32[2,128]{1,0:T(2,128)S(1)}, u32[]{:S(2)}, u32[]{:S(2)}) collective-permute-start(f32[2,128]{1,0:T(2,128)S(1)} %fusion.58), channel_id=1, source_target_pairs={{0,16},{1,17},{2,18},{3,19},{4,20},{5,21},{6,22},{7,23},{8,24},{9,... | collective-permute-start | bytes 3080 | tf_op jit(solution)/shard_map/ppermute | solution.py:32
  330.6 0.6 copy-start.10
  331.2 4.3 collective-permute-start.18
  335.5 0.6 copy-start.12
  336.1 5.8 %collective-permute-start.19 = (f32[2,128]{1,0:T(2,128)S(1)}, f32[2,128]{1,0:T(2,128)S(1)}, u32[]{:S(2)}, u32[]{:S(2)}) collective-permute-start(f32[2,128]{1,0:T(2,128)S(1)} %fusion.42), channel_id=1, source_target_pairs={{0,64},{1,65},{2,66},{3,67},{4,68},{5,69},{6,70},{7,71},{8,72},{9,... | collective-permute-start | bytes 3080 | tf_op jit(solution)/shard_map/ppermute | solution.py:32
  341.9 0.6 copy-start.14
  342.4 4.4 collective-permute-start.20
  347.6 7.0 %collective-permute-start.21 = (f32[2,128]{1,0:T(2,128)S(1)}, f32[2,128]{1,0:T(2,128)S(1)}, u32[]{:S(2)}, u32[]{:S(2)}) collective-permute-start(f32[2,128]{1,0:T(2,128)S(1)} %fusion.26), channel_id=1, source_target_pairs={{0,256},{1,257},{2,258},{3,259},{4,260},{5,261},{6,262},{7,263},{8... | collective-permute-start | bytes 3080 | tf_op jit(solution)/shard_map/ppermute | solution.py:32
  355.9 0.7 copy-start.15
  356.7 0.7 copy-start.13
  357.6 0.7 copy-start.11
  358.4 0.7 copy-start.9
  361.9 104.7 %copy-start.19 = (f32[2]{0:T(128)S(1)}, f32[2]{0:T(128)}, u32[]{:S(2)}) copy-start(f32[2]{0:T(128)} %copy-done.18) | copy-start | bytes 28
  466.6 0.7 copy-start.17
